TPU v7x, 32 devices: a whole 2x2x4 slice. The times are simulated.
32 devices in a mesh: parts: 2 (over y), shard: 2 (over core), blk: 8 (over z, x).
Axes of the slice: x: 2, y: 2, z: 4, core: 2. Of those that a mesh axis runs over, the one named last changes fastest.
Arguments:
- queries_in: bfloat16 [4096, 1024], P(('parts', 'shard', 'blk')), parts along dimension 0, may hold values from -12 to 12
- query_weight: bfloat16 [1024, 1024], replicated, may hold values from -0.1875 to 0.1875
- bank: bfloat16 [2048, 1024], P(('parts', 'shard', 'blk')), parts along dimension 0, may hold values from -110 to 110
- uses: int32 [4096, 2], P(('parts', 'shard', 'blk')), parts along dimension 0, may hold values from 0 to 1, as said below
Outputs:
- retrieved: bfloat16 [4096, 1024], P(('parts', 'shard', 'blk')), parts along dimension 0
There are 2 independent parts, one for each index of `parts`. A program takes and returns all parts, laid end to end along the dimension named above; an argument that names none is the same for every part. Nothing has to cross between parts.
Inputs may be any that keep to these rules, and one draw needn't show every extreme that they name: `uses`: every query lists one or both of the two shards. Of the 128 queries of one device, at most 128 list one shard, and in every draw for every index of blk the queries of both devices at that index all list one same shard.
All inputs are finite; a program needn't handle non-finite values.
Results may differ from a plain program's by a relative error of at most 0.035.
Values may be sent and summed in bfloat16 or wider, within the bound.
A program may use at most 128 MiB of HBM per device.

v0:
```python
import math
import jax
import jax.numpy as jnp
from jax import lax
from jax.sharding import PartitionSpec as P

HEADS = 8
HEAD_DIM = 128
NEGATIVE = -1e30


def empty_carry(slot_count):
    return (
        jnp.full((slot_count, HEADS), NEGATIVE, jnp.float32),
        jnp.zeros((slot_count, HEADS), jnp.float32),
        jnp.zeros((slot_count, HEADS, HEAD_DIM), jnp.float32),
    )


def fold_piece(carry, query_heads, piece, allowed):
    slot_count = query_heads.shape[0]
    piece_rows = piece.shape[0]
    key_rows = math.gcd(piece_rows, 512)
    key_blocks = piece_rows // key_rows
    keys_blocked = piece.reshape(key_blocks, key_rows, HEADS, HEAD_DIM)
    mask_blocked = allowed.reshape(slot_count, key_blocks, key_rows).transpose(1, 0, 2)
    block_rows = math.gcd(slot_count, 128)
    blocks = slot_count // block_rows
    logit_scale = HEAD_DIM ** (-0.5)

    def blocked(array):
        return array.reshape((blocks, block_rows) + array.shape[1:])

    def key_step(state, inputs):
        keys_piece, mask_all = inputs

        def one_block(block_inputs):
            query_block, mask_block, top_old, total_old, accum_old = block_inputs
            scores = (
                jnp.einsum(
                    "shd,rhd->shr", query_block, keys_piece, preferred_element_type=jnp.float32
                )
                * logit_scale
            )
            scores = jnp.where(mask_block[:, None, :], scores, NEGATIVE)
            top_new = jnp.maximum(top_old, jnp.max(scores, axis=-1))
            weights = jnp.where(mask_block[:, None, :], jnp.exp(scores - top_new[..., None]), 0.0)
            factor = jnp.exp(top_old - top_new)
            total_new = total_old * factor + jnp.sum(weights, axis=-1)
            accum_new = accum_old * factor[..., None] + jnp.einsum(
                "shr,rhd->shd",
                weights.astype(jnp.bfloat16),
                keys_piece,
                preferred_element_type=jnp.float32,
            )
            return (top_new, total_new, accum_new)

        top_old, total_old, accum_old = state
        results = lax.map(
            one_block,
            (
                blocked(query_heads),
                blocked(mask_all),
                blocked(top_old),
                blocked(total_old),
                blocked(accum_old),
            ),
        )
        return (
            tuple((result.reshape((slot_count,) + result.shape[2:]) for result in results)),
            None,
        )

    final, unused = lax.scan(key_step, carry, (keys_blocked, mask_blocked))
    return final


def local(queries_in, query_weight, bank, uses):
    row_count = queries_in.shape[0]
    width_all = HEADS * HEAD_DIM
    projected = jnp.dot(queries_in, query_weight, preferred_element_type=jnp.float32).astype(
        jnp.bfloat16
    )
    positions = jnp.cumsum(uses, axis=0) - 1
    listed = uses > 0
    onehot_table = (positions.T[:, None, :] == jnp.arange(row_count)[None, :, None]) & listed.T[
        :, None, :
    ]
    outgoing = jnp.einsum(
        "sct,td->scd",
        onehot_table.astype(jnp.bfloat16),
        projected,
        preferred_element_type=jnp.float32,
    ).astype(jnp.bfloat16)
    incoming = lax.all_to_all(outgoing, "shard", split_axis=0, concat_axis=0, tiled=True)
    item_count = incoming.shape[1]
    slot_heads = incoming.reshape(2 * item_count, HEADS, HEAD_DIM)
    piece = lax.all_gather(bank, "blk", axis=0, tiled=True)
    allowed = jnp.ones((2 * item_count, piece.shape[0]), dtype=jnp.bool_)
    top_part, total_part, accum_part = fold_piece(
        empty_carry(2 * item_count), slot_heads, piece, allowed
    )
    accum_back = lax.all_to_all(
        accum_part.reshape(2, item_count, width_all).astype(jnp.bfloat16),
        "shard",
        split_axis=0,
        concat_axis=0,
        tiled=True,
    ).astype(jnp.float32)
    top_back = lax.all_to_all(
        top_part.reshape(2, item_count, HEADS).astype(jnp.bfloat16),
        "shard",
        split_axis=0,
        concat_axis=0,
        tiled=True,
    ).astype(jnp.float32)
    total_back = lax.all_to_all(
        total_part.reshape(2, item_count, HEADS).astype(jnp.bfloat16),
        "shard",
        split_axis=0,
        concat_axis=0,
        tiled=True,
    ).astype(jnp.float32)
    safe_slot = jnp.clip(positions, 0, row_count - 1)
    top_pair = jnp.stack(
        [jnp.take(top_back[member], safe_slot[:, member], axis=0) for member in range(2)], 1
    )
    total_pair = jnp.stack(
        [jnp.take(total_back[member], safe_slot[:, member], axis=0) for member in range(2)], 1
    )
    accum_pair = jnp.stack(
        [jnp.take(accum_back[member], safe_slot[:, member], axis=0) for member in range(2)], 1
    )
    accum_pair = accum_pair.reshape(row_count, 2, HEADS, HEAD_DIM)
    top_pair = jnp.where(listed[:, :, None], top_pair, NEGATIVE)
    highest = jnp.max(top_pair, axis=1)
    scale_pair = jnp.where(listed[:, :, None], jnp.exp(top_pair - highest[:, None, :]), 0.0)
    total_all = jnp.sum(scale_pair * total_pair, axis=1)
    accum_all = jnp.sum(scale_pair[..., None] * accum_pair, axis=1)
    return (accum_all / total_all[..., None]).reshape(row_count, width_all).astype(jnp.bfloat16)


def solution(mesh):
    in_specs = (
        P(("parts", "shard", "blk"), None),
        P(),
        P(("parts", "shard", "blk"), None),
        P(("parts", "shard", "blk"), None),
    )
    out_specs = P(("parts", "shard", "blk"), None)
    return jax.shard_map(local, mesh=mesh, in_specs=in_specs, out_specs=out_specs, check_vma=False)
```

profile of v0, /device:TPU:1, one launch (start us, length us, event | category | flops | bytes accessed | tf_op | source)
XLA Modules:
  0.0 94.7 jit_solution(11347580435513448345)
XLA Ops:
  7.3 0.8 copy.41
  8.4 2.4 %convolution_convert_fusion = bf16[2,128,1024]{2,1,0:T(8,128)(2,1)} fusion(bf16[128,1024]{1,0:T(8,128)(2,1)} %param.10, bf16[1024,1024]{1,0:T(8,128)(2,1)S(1)} %copy-done, s32[2,128]{1,0:T(2,128)S(1)} %copy.44, pred[2,128]{1,0:T(4,128)(4,1)S(1)} %copy.45), kind=kOutput, calls=%fused_computation.29 | convolution fusion | flops 336003072 | bytes 2884864 | tf_op jit(solution)/shard_map/sct,td->scd/dot_general | solution.py:89
  10.8 3.5 %all-to-all-start = ((bf16[2,128,1024]{2,1,0:T(8,128)(2,1)}), bf16[2,128,1024]{2,1,0:T(8,128)(2,1)S(1)}, u32[]{:S(2)}, u32[]{:S(2)}) async-start(bf16[2,128,1024]{2,1,0:T(8,128)(2,1)} %convolution_convert_fusion), calls=%async_computation | async-start | bytes 1048576 | tf_op jit(solution)/shard_map/all_to_all | solution.py:95
  14.5 1.3 %all-to-all-done = bf16[2,128,1024]{2,1,0:T(8,128)(2,1)S(1)} async-done(((bf16[2,128,1024]{2,1,0:T(8,128)(2,1)}), bf16[2,128,1024]{2,1,0:T(8,128)(2,1)S(1)}, u32[]{:S(2)}, u32[]{:S(2)}) %all-to-all-start) | async-done | bytes 524320 | tf_op jit(solution)/shard_map/all_to_all | solution.py:95
  15.7 0.9 copy.60
  16.9 33.9 %all-gather.2.cloned.1.call-done = bf16[512,1024]{1,0:T(8,128)(2,1)} async-done(((bf16[64,1024]{1,0:T(8,128)(2,1)}), bf16[512,1024]{1,0:T(8,128)(2,1)}) %all-gather.2.cloned.1.call-update) | async-done | bytes 1048592 | tf_op jit(solution)/shard_map/all_gather | solution.py:98
  50.8 2.3 %copy.46 = bf16[512,1024]{0,1:T(8,128)(2,1)} copy(bf16[512,1024]{1,0:T(8,128)(2,1)} %all-gather.2.cloned.1.call-done) | data formatting | bytes 2097152 | tf_op jit(solution)/shard_map/all_gather | solution.py:98
  53.1 1.6 %copy.48 = bf16[512,8,128]{2,0,1:T(8,128)(2,1)S(1)} copy(bf16[512,8,128]{0,2,1:T(8,128)(2,1)} %bitcast.121) | data formatting | bytes 2097152 | tf_op jit(solution)/shard_map/while/body/eval_jaxpr/while | solution.py:59
  54.7 7.4 %while.26 = (s32[]{:T(128)}, bf16[2,128,8]{1,2,0:T(8,128)(2,1)S(1)}, bf16[2,128,8]{1,2,0:T(8,128)(2,1)}, bf16[2,128,8,128]{3,1,2,0:T(8,128)(2,1)}, bf16[2,128,8,...) while((s32[]{:T(128)}, bf16[2,128,8]{1,2,0:T(8,128)(2,1)S(1)}, ...), condition=%wide.region_4.5_spmd, body=%wide.region_1.4_spmd.sunk | while | flops 272768000 | bytes 13944989 | solution.py:59
  54.7 1.0 %constant_dynamic-slice_fusion.2 = bf16[1,128,8,128]{3,2,1,0:T(8,128)(2,1)S(1)} fusion(bf16[2,128,8,128]{3,2,1,0:T(8,128)(2,1)} %get-tuple-element.220, s32[]{:T(128)S(6)} %copy.80), kind=kLoop, calls=%fused_computation.27.clone.1 | loop fusion | bytes 524292 | tf_op jit(solution)/shard_map/while/body/eval_jaxpr/while/body/jit(dynamic_index_in_dim)/dynamic_slice | solution.py:59
  56.8 0.7 fusion.39
  58.4 1.0 %constant_dynamic-slice_fusion.2 = bf16[1,128,8,128]{3,2,1,0:T(8,128)(2,1)S(1)} fusion(bf16[2,128,8,128]{3,2,1,0:T(8,128)(2,1)} %get-tuple-element.220, s32[]{:T(128)S(6)} %copy.80), kind=kLoop, calls=%fused_computation.27.clone.1 | loop fusion | bytes 524292 | tf_op jit(solution)/shard_map/while/body/eval_jaxpr/while/body/jit(dynamic_index_in_dim)/dynamic_slice | solution.py:59
  60.5 0.7 fusion.39
  62.1 1.9 %copy_bitcast_fusion.2 = bf16[2,128,1024]{2,1,0:T(8,128)(2,1)} fusion(bf16[2,128,8,128]{3,1,2,0:T(8,128)(2,1)} %get-tuple-element.95), kind=kLoop, calls=%fused_computation.34 | loop fusion | bytes 1048576 | tf_op jit(solution)/shard_map/convert_element_type | solution.py:104
  64.0 5.0 %all_to_all.20 = bf16[2,128,8]{1,2,0:T(8,128)(2,1)S(1)} all-to-all(bf16[2,128,8]{1,2,0:T(8,128)(2,1)S(1)} %get-tuple-element.94), channel_id=1, replica_groups=mesh['parts'=2,'shard'=2,'blk'=8] {'shard'}, dimensions={0} | all-to-all | bytes 8192 | tf_op jit(solution)/shard_map/all_to_all | solution.py:110
  69.0 3.5 %all-to-all-start.3 = ((bf16[2,128,8]{1,2,0:T(8,128)(2,1)}), bf16[2,128,8]{1,2,0:T(8,128)(2,1)S(1)}, u32[]{:S(2)}, u32[]{:S(2)}) async-start(bf16[2,128,8]{1,2,0:T(8,128)(2,1)} %get-tuple-element.96), calls=%async_computation.3 | async-start | bytes 8192 | tf_op jit(solution)/shard_map/all_to_all | solution.py:117
  72.7 0.9 all-to-all-done.3
  73.6 3.8 %all-to-all-start.2 = ((bf16[2,128,1024]{2,1,0:T(8,128)(2,1)}), bf16[2,128,1024]{2,1,0:T(8,128)(2,1)S(1)}, u32[]{:S(2)}, u32[]{:S(2)}) async-start(bf16[2,128,1024]{2,1,0:T(8,128)(2,1)} %copy_bitcast_fusion.2), calls=%async_computation.2 | async-start | bytes 1048576 | tf_op jit(solution)/shard_map/all_to_all | solution.py:103
  81.0 1.6 %gather_fusion.2 = f32[128,1024]{1,0:T(8,128)} fusion(f32[128,1024]{1,0:T(8,128)S(1)} %get-tuple-element.141, s32[1024]{0:T(1024)S(1)} %pad_clamp_fusion.1), kind=kCustom, calls=%fused_computation.1.clone | custom fusion | bytes 1049088 | tf_op jit(solution)/shard_map/jit(_take)/gather | solution.py:132
  82.6 1.1 %select_bitcast_fusion.1 = f32[16,8,8,128]{3,1,2,0:T(8,128)S(1)} fusion(f32[128,1024]{1,0:T(8,128)} %gather_fusion.2, pred[128]{0:T(512)(128)(4,1)S(1)} %get-tuple-element.156), kind=kLoop, calls=%fused_computation.38 | loop fusion | flops 131072 | bytes 1048704
  83.8 0.9 copy.61
  84.7 0.8 gather_fusion.3
  85.7 0.8 copy-done.1
  87.1 0.8 copy.70
  (65 shorter events, 9.7 us)
Async XLA Ops:
  6.5 1.9 %copy-start = (bf16[1024,1024]{1,0:T(8,128)(2,1)S(1)}, bf16[1024,1024]{1,0:T(8,128)(2,1)}, u32[]{:S(2)}) copy-start(bf16[1024,1024]{1,0:T(8,128)(2,1)} %param.11) | copy-start | bytes 6291460
  6.5 44.3 %all-gather.2.cloned.1.call-start = ((), (), s32[]{:S(2)}) async-start(), calls=%async_computation.4 | async-start | bytes 1179648 | tf_op jit(solution)/shard_map/all_gather | solution.py:98
  10.8 4.9 %all-to-all-start = ((bf16[2,128,1024]{2,1,0:T(8,128)(2,1)}), bf16[2,128,1024]{2,1,0:T(8,128)(2,1)S(1)}, u32[]{:S(2)}, u32[]{:S(2)}) async-start(bf16[2,128,1024]{2,1,0:T(8,128)(2,1)} %convolution_convert_fusion), calls=%async_computation | async-start | bytes 1048576 | tf_op jit(solution)/shard_map/all_to_all | solution.py:95
  55.7 1.1 %copy-start.2 = (bf16[2,128,8,128]{3,1,2,0:T(8,128)(2,1)S(1)}, bf16[2,128,8,128]{3,1,2,0:T(8,128)(2,1)}, u32[]{:S(2)}) copy-start(bf16[2,128,8,128]{3,1,2,0:T(8,128)(2,1)} %get-tuple-element.212) | copy-start | bytes 1572868 | tf_op jit(solution)/shard_map/while/body/eval_jaxpr/while
  57.6 0.8 copy-start.3
  59.4 1.1 %copy-start.2 = (bf16[2,128,8,128]{3,1,2,0:T(8,128)(2,1)S(1)}, bf16[2,128,8,128]{3,1,2,0:T(8,128)(2,1)}, u32[]{:S(2)}) copy-start(bf16[2,128,8,128]{3,1,2,0:T(8,128)(2,1)} %get-tuple-element.212) | copy-start | bytes 1572868 | tf_op jit(solution)/shard_map/while/body/eval_jaxpr/while
  61.3 0.8 copy-start.3
  69.0 4.6 %all-to-all-start.3 = ((bf16[2,128,8]{1,2,0:T(8,128)(2,1)}), bf16[2,128,8]{1,2,0:T(8,128)(2,1)S(1)}, u32[]{:S(2)}, u32[]{:S(2)}) async-start(bf16[2,128,8]{1,2,0:T(8,128)(2,1)} %get-tuple-element.96), calls=%async_computation.3 | async-start | bytes 8192 | tf_op jit(solution)/shard_map/all_to_all | solution.py:117
  73.6 7.3 %all-to-all-start.2 = ((bf16[2,128,1024]{2,1,0:T(8,128)(2,1)}), bf16[2,128,1024]{2,1,0:T(8,128)(2,1)S(1)}, u32[]{:S(2)}, u32[]{:S(2)}) async-start(bf16[2,128,1024]{2,1,0:T(8,128)(2,1)} %copy_bitcast_fusion.2), calls=%async_computation.2 | async-start | bytes 1048576 | tf_op jit(solution)/shard_map/all_to_all | solution.py:103
  85.5 1.0 %copy-start.1 = (f32[16,8,8,128]{3,2,1,0:T(8,128)S(1)}, f32[16,8,8,128]{3,2,1,0:T(8,128)}, u32[]{:S(2)}) copy-start(f32[16,8,8,128]{3,2,1,0:T(8,128)} %copy.61) | copy-start | bytes 1572868
Sparse Core Ops, SparseCore 0:
  9.5 41.2 all-gather.1
where the time goes:
time: 95.3 us; the launch traced here: 94.7 us
  waiting for transfers between devices  36.8 us (39%)
  local copies, waits for them, and re-layouts  18.4 us (19%)
  between operations  13.6 us (14%)
  starting transfers between devices  10.9 us (11%)
  blocking collectives  5.01 us (5%)
  matrix products  4.94 us (5%)
  other arithmetic  4.87 us (5%)
    all_gather x1, waiting for transfers between devices, local(): piece = lax.all_gather(bank, 'blk', axis=0, tiled=True)  33.9 us
    all_to_all x1, blocking collectives, local(): lax.all_to_all(top_part.reshape(2, item_count, HEADS).astype(jnp.bfloat16...  5.01 us
    unnamed x9, local copies, waits for them, and re-layouts  4.23 us
    all_to_all x1, starting transfers between devices, local(): lax.all_to_all(accum_part.reshape(2, item_count, width_all).astype(jnp.bf...  3.81 us
    all_to_all x1, starting transfers between devices, local(): lax.all_to_all(total_part.reshape(2, item_count, HEADS).astype(jnp.bfloat...  3.55 us
    all_to_all x1, starting transfers between devices, local(): lax.all_to_all(outgoing, 'shard', split_axis=0, concat_axis=0, tiled=True)  3.53 us
    dot_general x1, matrix products, local(): jnp.einsum('sct,td->scd', onehot_table.astype(jnp.bfloat16), projected, p...  2.43 us
    gather x2, local copies, waits for them, and re-layouts, local(): jnp.take(accum_back[member], safe_slot[:, member], axis=0)  2.38 us
  transfers between devices with their start and end apart: 4, of which 3 were waited for; matrix products, arithmetic and copies ran while one was open for 9% of the time, Pallas kernels for 0%

commit v1 on v0

--- a/solution.py
+++ b/solution.py
@@ -1,3 +1,4 @@
+import functools
 import math
 import jax
 import jax.numpy as jnp
@@ -7,6 +8,34 @@
 HEADS = 8
 HEAD_DIM = 128
 NEGATIVE = -1e30
+
+
+def draft_the_face(s0, d_out):
+    a_next = list(s0.shape[1:])
+    a_next[d_out] *= s0.shape[0]
+    return jnp.moveaxis(s0, 0, d_out).reshape(a_next)
+
+
+def check_the_local_data(shard_in, device_axis):
+    n_parts = lax.axis_size(device_axis)
+    piece_out = shard_in[None]
+    for at in range(n_parts.bit_length() - 1):
+        n_now = 1 << at
+        chunks = []
+        for i in tuple(range(n_parts)):
+            chunks.append((i, i ^ n_now))
+        current_arr = lax.ppermute(piece_out, device_axis, chunks)
+        arr_out = jnp.stack([piece_out, current_arr])
+        small = lax.axis_index(device_axis) >> at & 1
+        piece_out = jnp.where(small == 0, arr_out, arr_out[::-1]).reshape(-1, *shard_in.shape)
+    return piece_out
+
+
+def open_streams_here(here_x, array_here, in_dim):
+    return draft_the_face(check_the_local_data(here_x, array_here), in_dim)
+
+
+write_ways_on_mesh = functools.partial(open_streams_here, array_here="blk", in_dim=0)
 
 
 def empty_carry(slot_count):
@@ -95,7 +124,7 @@
     incoming = lax.all_to_all(outgoing, "shard", split_axis=0, concat_axis=0, tiled=True)
     item_count = incoming.shape[1]
     slot_heads = incoming.reshape(2 * item_count, HEADS, HEAD_DIM)
-    piece = lax.all_gather(bank, "blk", axis=0, tiled=True)
+    piece = write_ways_on_mesh(bank)
     allowed = jnp.ones((2 * item_count, piece.shape[0]), dtype=jnp.bool_)
     top_part, total_part, accum_part = fold_piece(
         empty_carry(2 * item_count), slot_heads, piece, allowed

time: 95.3 us -> 78.9 us (0.83)
  between operations: 13.6 us -> 0.28 us
  waiting for transfers between devices: 36.8 us -> 28.3 us
  starting transfers between devices: 10.9 us -> 17.6 us
  local copies, waits for them, and re-layouts: 18.4 us -> 15.6 us
  other arithmetic: 4.87 us -> 6.52 us
    all_gather x1 -> x0, waiting for transfers between devices: 33.9 us -> none  [local(): piece = lax.all_gather(bank, 'blk', axis=0, tiled=True)]
    ppermute x0 -> x3, waiting for transfers between devices: none -> 27.5 us  [check_the_local_data(): current_arr = lax.ppermute(piece_out, device_axis, chunks)]
    ppermute x0 -> x3, starting transfers between devices: none -> 5.78 us  [check_the_local_data(): current_arr = lax.ppermute(piece_out, device_axis, chunks)]
    all_gather x1 -> x0, local copies, waits for them, and re-layouts: 2.28 us -> none  [local(): piece = lax.all_gather(bank, 'blk', axis=0, tiled=True)]
    while x1, local copies, waits for them, and re-layouts: 1.61 us -> 0.14 us  [key_step(): lax.map(one_block, (blocked(query_heads), blocked(mask_all), blocked(top_...]
    another operation x3 -> x7, other arithmetic: 0.01 us -> 1.29 us  [the longest x4 1.28 us: check_the_local_data(): arr_out = jnp.stack([piece_out, current_arr])]
    all_to_all x1, waiting for transfers between devices: 1.28 us -> 0.01 us  [local(): lax.all_to_all(outgoing, 'shard', split_axis=0, concat_axis=0, tiled=True)]
    unnamed x9 -> x20, local copies, waits for them, and re-layouts: 4.23 us -> 4.57 us
  transfers between devices with their start and end apart: 4 -> 6, of which waited for: 3 -> 3; matrix products, arithmetic and copies ran while one was open for 9% -> 12% of each run, Pallas kernels for 0% -> 0%
where the time goes in v1:
time: 78.9 us; the launch traced here: 78.3 us
  waiting for transfers between devices  28.3 us (36%)
  starting transfers between devices  17.6 us (22%)
  local copies, waits for them, and re-layouts  15.6 us (20%)
  other arithmetic  6.52 us (8%)
  matrix products  4.95 us (6%)
  blocking collectives  4.89 us (6%)
    ppermute x3, waiting for transfers between devices, check_the_local_data(): current_arr = lax.ppermute(piece_out, device_axis, chunks)  27.5 us
    ppermute x3, starting transfers between devices, check_the_local_data(): current_arr = lax.ppermute(piece_out, device_axis, chunks)  5.78 us
    all_to_all x1, blocking collectives, local(): lax.all_to_all(top_part.reshape(2, item_count, HEADS).astype(jnp.bfloat16...  4.89 us
    unnamed x20, local copies, waits for them, and re-layouts  4.57 us
    all_to_all x1, starting transfers between devices, local(): lax.all_to_all(outgoing, 'shard', split_axis=0, concat_axis=0, tiled=True)  4.43 us
    all_to_all x1, starting transfers between devices, local(): lax.all_to_all(accum_part.reshape(2, item_count, width_all).astype(jnp.bf...  3.81 us
    all_to_all x1, starting transfers between devices, local(): lax.all_to_all(total_part.reshape(2, item_count, HEADS).astype(jnp.bfloat...  3.55 us
    dot_general x1, matrix products, local(): jnp.einsum('sct,td->scd', onehot_table.astype(jnp.bfloat16), projected, p...  2.43 us
  transfers between devices with their start and end apart: 6, of which 3 were waited for; matrix products, arithmetic and copies ran while one was open for 12% of the time, Pallas kernels for 0%

profile of v1, /device:TPU:1, one launch (start us, length us, event | category | flops | bytes accessed | tf_op | source)
XLA Modules:
  0.0 78.3 jit_solution(8117542033250080453)
XLA Ops:
  0.0 2.0 %collective-permute-start = (bf16[1,64,1024]{2,1,0:T(8,128)(2,1)}, bf16[1,64,1024]{2,1,0:T(8,128)(2,1)S(1)}, u32[]{:S(2)}, u32[]{:S(2)}) collective-permute-start(bf16[1,64,1024]{2,1,0:T(8,128)(2,1)} %bitcast.144), channel_id=1, source_target_pairs={{0,1},{1,0},{2,3},{3,2},{4,5},{5,4},{6,7},{7,6},{8,9},{9,8},{10,11... | collective-permute-start | bytes 393224 | tf_op jit(solution)/shard_map/ppermute | solution.py:27
  2.0 0.8 %copy.39 = s32[128,2]{1,0:T(8,128)S(1)} copy(s32[128,2]{0,1:T(2,128)} %param.13) | data formatting | bytes 2048 | tf_op args[3]
  3.2 2.4 %convolution_convert_fusion = bf16[2,128,1024]{2,1,0:T(8,128)(2,1)} fusion(bf16[128,1024]{1,0:T(8,128)(2,1)} %param.10, bf16[1024,1024]{1,0:T(8,128)(2,1)S(1)} %copy-done, s32[2,128]{1,0:T(2,128)S(1)} %copy.42, pred[2,128]{1,0:T(4,128)(4,1)S(1)} %copy.43), kind=kOutput, calls=%fused_computation.30 | convolution fusion | flops 336003072 | bytes 2884864 | tf_op jit(solution)/shard_map/sct,td->scd/dot_general | solution.py:118
  5.6 4.4 %all-to-all-start = ((bf16[2,128,1024]{2,1,0:T(8,128)(2,1)}), bf16[2,128,1024]{2,1,0:T(8,128)(2,1)S(1)}, u32[]{:S(2)}, u32[]{:S(2)}) async-start(bf16[2,128,1024]{2,1,0:T(8,128)(2,1)} %convolution_convert_fusion), calls=%async_computation | async-start | bytes 1048576 | tf_op jit(solution)/shard_map/all_to_all | solution.py:124
  10.2 1.4 %collective-permute-start.1 = (bf16[2,64,1024]{2,1,0:T(8,128)(2,1)S(1)}, bf16[2,64,1024]{2,1,0:T(8,128)(2,1)S(1)}, u32[]{:S(2)}, u32[]{:S(2)}) collective-permute-start(bf16[2,64,1024]{2,1,0:T(8,128)(2,1)S(1)} %get-tuple-element.144), channel_id=1, source_target_pairs={{0,2},{1,3},{2,0},{3,1},{4,6},{5,7},{6,4},{7,5},{8,10},{9,11},{10,... | collective-permute-start | bytes 786440 | tf_op jit(solution)/shard_map/ppermute | solution.py:27
  12.3 5.8 %collective-permute-done.1 = bf16[2,64,1024]{2,1,0:T(8,128)(2,1)S(1)} collective-permute-done((bf16[2,64,1024]{2,1,0:T(8,128)(2,1)S(1)}, bf16[2,64,1024]{2,1,0:T(8,128)(2,1)S(1)}, u32[]{:S(2)}, u32[]{:S(2)}) %collective-permute-start.1) | collective-permute-done | bytes 262176 | tf_op jit(solution)/shard_map/ppermute | solution.py:27
  18.3 2.4 %collective-permute-start.2 = (bf16[4,64,1024]{2,1,0:T(8,128)(2,1)S(1)}, bf16[4,64,1024]{2,1,0:T(8,128)(2,1)}, u32[]{:S(2)}, u32[]{:S(2)}) collective-permute-start(bf16[4,64,1024]{2,1,0:T(8,128)(2,1)S(1)} %bitcast.140), channel_id=1, source_target_pairs={{0,4},{1,5},{2,6},{3,7},{4,0},{5,1},{6,2},{7,3},{8,12},{9,13},{10,... | collective-permute-start | bytes 1572872 | tf_op jit(solution)/shard_map/ppermute | solution.py:27
  20.8 0.9 %copy.57 = bf16[32,8,8,128]{3,2,1,0:T(8,128)(2,1)} copy(bf16[32,8,8,128]{3,1,2,0:T(8,128)(2,1)S(1)} %bitcast.137) | data formatting | bytes 1048576
  21.8 21.6 %collective-permute-done.2 = bf16[4,64,1024]{2,1,0:T(8,128)(2,1)} collective-permute-done((bf16[4,64,1024]{2,1,0:T(8,128)(2,1)S(1)}, bf16[4,64,1024]{2,1,0:T(8,128)(2,1)}, u32[]{:S(2)}, u32[]{:S(2)}) %collective-permute-start.2) | collective-permute-done | bytes 524320 | tf_op jit(solution)/shard_map/ppermute | solution.py:27
  43.4 1.1 %pad_maximum_fusion = bf16[2,4,64,1024]{3,2,1,0:T(8,128)(2,1)S(1)} fusion(bf16[1,4,64,1024]{3,2,1,0:T(8,128)(2,1)} %bitcast.17, bf16[1,4,64,1024]{3,2,1,0:T(8,128)(2,1)S(1)} %bitcast.141), kind=kLoop, calls=%fused_computation.33 | loop fusion | flops 524288 | bytes 2097152 | tf_op jit(solution)/shard_map/stack | solution.py:28
  45.2 7.4 %while.26 = (s32[]{:T(128)}, bf16[2,128,8]{1,2,0:T(8,128)(2,1)S(1)}, bf16[2,128,8]{1,2,0:T(8,128)(2,1)}, bf16[2,128,8,128]{3,1,2,0:T(8,128)(2,1)}, bf16[2,128,8,...) while((s32[]{:T(128)}, bf16[2,128,8]{1,2,0:T(8,128)(2,1)S(1)}, ...), condition=%wide.region_4.5_spmd, body=%wide.region_1.4_spmd.sunk | while | flops 272768000 | bytes 13944989 | solution.py:88
  45.3 1.0 %constant_dynamic-slice_fusion.2 = bf16[1,128,8,128]{3,2,1,0:T(8,128)(2,1)S(1)} fusion(bf16[2,128,8,128]{3,2,1,0:T(8,128)(2,1)} %get-tuple-element.222, s32[]{:T(128)S(6)} %copy.78), kind=kLoop, calls=%fused_computation.27.clone.1 | loop fusion | bytes 524292 | tf_op jit(solution)/shard_map/while/body/eval_jaxpr/while/body/jit(dynamic_index_in_dim)/dynamic_slice | solution.py:88
  48.9 1.0 %constant_dynamic-slice_fusion.2 = bf16[1,128,8,128]{3,2,1,0:T(8,128)(2,1)S(1)} fusion(bf16[2,128,8,128]{3,2,1,0:T(8,128)(2,1)} %get-tuple-element.222, s32[]{:T(128)S(6)} %copy.78), kind=kLoop, calls=%fused_computation.27.clone.1 | loop fusion | bytes 524292 | tf_op jit(solution)/shard_map/while/body/eval_jaxpr/while/body/jit(dynamic_index_in_dim)/dynamic_slice | solution.py:88
  52.6 1.9 %copy_bitcast_fusion.2 = bf16[2,128,1024]{2,1,0:T(8,128)(2,1)} fusion(bf16[2,128,8,128]{3,1,2,0:T(8,128)(2,1)} %get-tuple-element.95), kind=kLoop, calls=%fused_computation.37 | loop fusion | bytes 1048576 | tf_op jit(solution)/shard_map/convert_element_type | solution.py:133
  54.5 4.9 %all_to_all.20 = bf16[2,128,8]{1,2,0:T(8,128)(2,1)S(1)} all-to-all(bf16[2,128,8]{1,2,0:T(8,128)(2,1)S(1)} %get-tuple-element.94), channel_id=1, replica_groups=mesh['parts'=2,'shard'=2,'blk'=8] {'shard'}, dimensions={0} | all-to-all | bytes 8192 | tf_op jit(solution)/shard_map/all_to_all | solution.py:139
  59.4 3.5 %all-to-all-start.3 = ((bf16[2,128,8]{1,2,0:T(8,128)(2,1)}), bf16[2,128,8]{1,2,0:T(8,128)(2,1)S(1)}, u32[]{:S(2)}, u32[]{:S(2)}) async-start(bf16[2,128,8]{1,2,0:T(8,128)(2,1)} %get-tuple-element.96), calls=%async_computation.3 | async-start | bytes 8192 | tf_op jit(solution)/shard_map/all_to_all | solution.py:146
  63.1 0.9 %all-to-all-done.3 = bf16[2,128,8]{1,2,0:T(8,128)(2,1)S(1)} async-done(((bf16[2,128,8]{1,2,0:T(8,128)(2,1)}), bf16[2,128,8]{1,2,0:T(8,128)(2,1)S(1)}, u32[]{:S(2)}, u32[]{:S(2)}) %all-to-all-start.3) | async-done | bytes 4128 | tf_op jit(solution)/shard_map/all_to_all | solution.py:146
  64.0 3.8 %all-to-all-start.2 = ((bf16[2,128,1024]{2,1,0:T(8,128)(2,1)}), bf16[2,128,1024]{2,1,0:T(8,128)(2,1)S(1)}, u32[]{:S(2)}, u32[]{:S(2)}) async-start(bf16[2,128,1024]{2,1,0:T(8,128)(2,1)} %copy_bitcast_fusion.2), calls=%async_computation.2 | async-start | bytes 1048576 | tf_op jit(solution)/shard_map/all_to_all | solution.py:132
  71.5 1.6 %gather_fusion.2 = f32[128,1024]{1,0:T(8,128)} fusion(f32[128,1024]{1,0:T(8,128)S(1)} %get-tuple-element.141, s32[1024]{0:T(1024)S(1)} %pad_clamp_fusion.1), kind=kCustom, calls=%fused_computation.1.clone | custom fusion | bytes 1049088 | tf_op jit(solution)/shard_map/jit(_take)/gather | solution.py:161
  73.1 1.1 %select_bitcast_fusion.1 = f32[16,8,8,128]{3,1,2,0:T(8,128)S(1)} fusion(f32[128,1024]{1,0:T(8,128)} %gather_fusion.2, pred[128]{0:T(512)(128)(4,1)S(1)} %get-tuple-element.158), kind=kLoop, calls=%fused_computation.42 | loop fusion | flops 131072 | bytes 1048704
  74.2 0.9 %copy.59 = f32[16,8,8,128]{3,2,1,0:T(8,128)} copy(f32[16,8,8,128]{3,1,2,0:T(8,128)S(1)} %select_bitcast_fusion.1) | data formatting | bytes 1048576
  75.1 0.8 %gather_fusion.3 = f32[128,1024]{1,0:T(8,128)S(1)} fusion(f32[128,1024]{1,0:T(8,128)S(1)} %get-tuple-element.142, s32[1024]{0:T(1024)S(1)} %pad_clamp_fusion), kind=kCustom, calls=%fused_computation.5.clone | custom fusion | bytes 1049088 | tf_op jit(solution)/shard_map/jit(_take)/gather | solution.py:161
  76.1 0.8 %copy-done.1 = f32[16,8,8,128]{3,2,1,0:T(8,128)S(1)} copy-done((f32[16,8,8,128]{3,2,1,0:T(8,128)S(1)}, f32[16,8,8,128]{3,2,1,0:T(8,128)}, u32[]{:S(2)}) %copy-start.1) | copy-done | bytes 524312
  77.5 0.8 copy.68
  (84 shorter events, 11.9 us)
Async XLA Ops:
  0.0 3.2 %copy-start = (bf16[1024,1024]{1,0:T(8,128)(2,1)S(1)}, bf16[1024,1024]{1,0:T(8,128)(2,1)}, u32[]{:S(2)}) copy-start(bf16[1024,1024]{1,0:T(8,128)(2,1)} %param.11) | copy-start | bytes 6291460
  0.0 10.1 %collective-permute-start = (bf16[1,64,1024]{2,1,0:T(8,128)(2,1)}, bf16[1,64,1024]{2,1,0:T(8,128)(2,1)S(1)}, u32[]{:S(2)}, u32[]{:S(2)}) collective-permute-start(bf16[1,64,1024]{2,1,0:T(8,128)(2,1)} %bitcast.144), channel_id=1, source_target_pairs={{0,1},{1,0},{2,3},{3,2},{4,5},{5,4},{6,7},{7,6},{8,9},{9,8},{10,11... | collective-permute-start | bytes 393224 | tf_op jit(solution)/shard_map/ppermute | solution.py:27
  3.1 7.0 %copy-start.4 = (bf16[64,1024]{1,0:T(8,128)(2,1)S(1)}, bf16[64,1024]{1,0:T(8,128)(2,1)}, u32[]{:S(2)}) copy-start(bf16[64,1024]{1,0:T(8,128)(2,1)} %param.12) | copy-start | bytes 393220
  5.6 15.2 %all-to-all-start = ((bf16[2,128,1024]{2,1,0:T(8,128)(2,1)}), bf16[2,128,1024]{2,1,0:T(8,128)(2,1)S(1)}, u32[]{:S(2)}, u32[]{:S(2)}) async-start(bf16[2,128,1024]{2,1,0:T(8,128)(2,1)} %convolution_convert_fusion), calls=%async_computation | async-start | bytes 1048576 | tf_op jit(solution)/shard_map/all_to_all | solution.py:124
  10.2 8.0 %collective-permute-start.1 = (bf16[2,64,1024]{2,1,0:T(8,128)(2,1)S(1)}, bf16[2,64,1024]{2,1,0:T(8,128)(2,1)S(1)}, u32[]{:S(2)}, u32[]{:S(2)}) collective-permute-start(bf16[2,64,1024]{2,1,0:T(8,128)(2,1)S(1)} %get-tuple-element.144), channel_id=1, source_target_pairs={{0,2},{1,3},{2,0},{3,1},{4,6},{5,7},{6,4},{7,5},{8,10},{9,11},{10,... | collective-permute-start | bytes 786440 | tf_op jit(solution)/shard_map/ppermute | solution.py:27
  12.3 8.4 %copy-start.5 = (s32[128]{0:T(128)S(1)}, s32[128]{0:T(128)}, u32[]{:S(2)}) copy-start(s32[128]{0:T(128)} %get-tuple-element.121) | copy-start | bytes 1540
  12.3 8.4 %copy-start.7 = (s32[128]{0:T(128)S(1)}, s32[128]{0:T(128)}, u32[]{:S(2)}) copy-start(s32[128]{0:T(128)} %get-tuple-element.122) | copy-start | bytes 1540
  18.1 3.6 %copy-start.6 = (s32[128]{0:T(128)S(1)}, s32[128]{0:T(128)}, u32[]{:S(2)}) copy-start(s32[128]{0:T(128)} %get-tuple-element.121) | copy-start | bytes 1540
  18.1 3.6 %copy-start.8 = (s32[128]{0:T(128)S(1)}, s32[128]{0:T(128)}, u32[]{:S(2)}) copy-start(s32[128]{0:T(128)} %get-tuple-element.122) | copy-start | bytes 1540
  18.3 25.1 %collective-permute-start.2 = (bf16[4,64,1024]{2,1,0:T(8,128)(2,1)S(1)}, bf16[4,64,1024]{2,1,0:T(8,128)(2,1)}, u32[]{:S(2)}, u32[]{:S(2)}) collective-permute-start(bf16[4,64,1024]{2,1,0:T(8,128)(2,1)S(1)} %bitcast.140), channel_id=1, source_target_pairs={{0,4},{1,5},{2,6},{3,7},{4,0},{5,1},{6,2},{7,3},{8,12},{9,13},{10,... | collective-permute-start | bytes 1572872 | tf_op jit(solution)/shard_map/ppermute | solution.py:27
  46.2 1.1 %copy-start.2 = (bf16[2,128,8,128]{3,1,2,0:T(8,128)(2,1)S(1)}, bf16[2,128,8,128]{3,1,2,0:T(8,128)(2,1)}, u32[]{:S(2)}) copy-start(bf16[2,128,8,128]{3,1,2,0:T(8,128)(2,1)} %get-tuple-element.214) | copy-start | bytes 1572868 | tf_op jit(solution)/shard_map/while/body/eval_jaxpr/while
  48.1 0.8 %copy-start.3 = (bf16[2,128,8,128]{3,1,2,0:T(8,128)(2,1)}, bf16[2,128,8,128]{3,1,2,0:T(8,128)(2,1)S(1)}, u32[]{:S(2)}) copy-start(bf16[2,128,8,128]{3,1,2,0:T(8,128)(2,1)S(1)} %fusion.41) | copy-start | bytes 1572868 | tf_op jit(solution)/shard_map/while/body/eval_jaxpr/while
  49.9 1.1 %copy-start.2 = (bf16[2,128,8,128]{3,1,2,0:T(8,128)(2,1)S(1)}, bf16[2,128,8,128]{3,1,2,0:T(8,128)(2,1)}, u32[]{:S(2)}) copy-start(bf16[2,128,8,128]{3,1,2,0:T(8,128)(2,1)} %get-tuple-element.214) | copy-start | bytes 1572868 | tf_op jit(solution)/shard_map/while/body/eval_jaxpr/while
  51.8 0.8 %copy-start.3 = (bf16[2,128,8,128]{3,1,2,0:T(8,128)(2,1)}, bf16[2,128,8,128]{3,1,2,0:T(8,128)(2,1)S(1)}, u32[]{:S(2)}) copy-start(bf16[2,128,8,128]{3,1,2,0:T(8,128)(2,1)S(1)} %fusion.41) | copy-start | bytes 1572868 | tf_op jit(solution)/shard_map/while/body/eval_jaxpr/while
  59.4 4.6 %all-to-all-start.3 = ((bf16[2,128,8]{1,2,0:T(8,128)(2,1)}), bf16[2,128,8]{1,2,0:T(8,128)(2,1)S(1)}, u32[]{:S(2)}, u32[]{:S(2)}) async-start(bf16[2,128,8]{1,2,0:T(8,128)(2,1)} %get-tuple-element.96), calls=%async_computation.3 | async-start | bytes 8192 | tf_op jit(solution)/shard_map/all_to_all | solution.py:146
  64.0 7.3 %all-to-all-start.2 = ((bf16[2,128,1024]{2,1,0:T(8,128)(2,1)}), bf16[2,128,1024]{2,1,0:T(8,128)(2,1)S(1)}, u32[]{:S(2)}, u32[]{:S(2)}) async-start(bf16[2,128,1024]{2,1,0:T(8,128)(2,1)} %copy_bitcast_fusion.2), calls=%async_computation.2 | async-start | bytes 1048576 | tf_op jit(solution)/shard_map/all_to_all | solution.py:132
  75.9 1.0 %copy-start.1 = (f32[16,8,8,128]{3,2,1,0:T(8,128)S(1)}, f32[16,8,8,128]{3,2,1,0:T(8,128)}, u32[]{:S(2)}) copy-start(f32[16,8,8,128]{3,2,1,0:T(8,128)} %copy.59) | copy-start | bytes 1572868
